TPU v7x, 32 devices: a whole 2x2x4 slice. The times are simulated.
32 devices in a mesh: parts: 2 (over x), dp: 16 (over z, y, core).
Axes of the slice: x: 2, y: 2, z: 4, core: 2. Of those that a mesh axis runs over, the one named last changes fastest.
Arguments:
- grads: bfloat16 [2048, 3, 10240], P(('parts', 'dp')), parts along dimension 0, may hold values from -4 to 4
- valid: bfloat16 [32, 3, 10240], P(('parts', 'dp')), parts along dimension 0, may hold values from -6 to 6
Outputs:
- weighted: float32 [32, 3, 10240], P(('parts', 'dp')), parts along dimension 0
There are 2 independent parts, one for each index of `parts`. A program takes and returns all parts, laid end to end along the dimension named above; each array names one. Nothing has to cross between parts.
All inputs are finite; a program needn't handle non-finite values.
Results may differ from a plain program's by a relative error of at most 0.0026.
Values may be sent and summed in bfloat16 or wider, within the bound.
A program may use at most 64 MiB of HBM per device.

v0:
```python
import jax
import jax.numpy as jnp
from jax import lax
from jax.sharding import PartitionSpec as P


def coefficients(grads, block, damping, norms):
    dots = jnp.einsum("elw,vlw->lev", grads, block, preferred_element_type=jnp.float32)
    return (dots / (damping[:, None, None] + norms.T[:, :, None])).astype(jnp.bfloat16)


def shards(grads, valid):
    local_rows = grads.shape[0]
    norms = jnp.einsum("elw,elw->el", grads, grads, preferred_element_type=jnp.float32)
    total = lax.psum(jnp.sum(norms, axis=0), "dp")
    damping = 0.1 * total / (local_rows * lax.axis_size("dp"))
    everything = lax.all_gather(valid, "dp", axis=0, tiled=True)
    coef = coefficients(grads, everything, damping, norms)
    return lax.psum_scatter(
        jnp.einsum("lev,elw->vlw", coef, grads, preferred_element_type=jnp.float32),
        "dp",
        scatter_dimension=0,
        tiled=True,
    )


def solution(mesh):
    return jax.shard_map(
        shards,
        mesh=mesh,
        in_specs=(P(("parts", "dp"), None, None), P(("parts", "dp"), None, None)),
        out_specs=P(("parts", "dp"), None, None),
        check_vma=False,
    )
```

profile of v0, /device:TPU:0, one launch (start us, length us, event | category | flops | bytes accessed | tf_op | source)
XLA Modules:
  0.0 182.9 jit_solution(16031383538184144877)
XLA Ops:
  6.5 0.0 copy-start
  6.5 0.0 all-reduce.3.cloned.1.call-start
  6.5 3.0 %fusion = f32[64,3]{0,1:T(4,128)S(1)} fusion(bf16[64,3,10240]{2,0,1:T(8,128)(2,1)} %param.2), kind=kLoop, calls=%fused_computation.2 | loop fusion | flops 5898048 | bytes 3932928 | tf_op jit(solution)/shard_map/elw,elw->el/dot_general | solution.py:14
  9.6 0.1 reduce_sum.9
  9.7 35.0 %psum.7 = f32[3]{0:T(128)S(1)} all-reduce(f32[3]{0:T(128)S(1)} %reduce_sum.9), channel_id=1, replica_groups=mesh['parts'=2,'dp'=16] {'dp'}, use_global_device_ids=true, to_apply=%region_1.0 | all-reduce | flops 3 | bytes 24 | tf_op jit(solution)/shard_map/psum | solution.py:15
  44.7 0.1 add_bitcast_fusion
  44.8 0.0 copy-done
  44.8 22.8 %all_gather.3 = bf16[16,3,10240]{2,1,0:T(4,128)(2,1)S(1)} all-gather(bf16[1,3,10240]{2,1,0:T(4,128)(2,1)S(1)} %copy-done), channel_id=1, replica_groups=mesh['parts'=2,'dp'=16] {'dp'}, dimensions={0}, use_global_device_ids=true | all-gather | bytes 1044480 | tf_op jit(solution)/shard_map/all_gather | solution.py:17
  67.5 5.1 %convolution_bitcast_fusion = f32[16,3,10240]{2,0,1:T(8,128)S(1)} fusion(bf16[64,3,10240]{2,0,1:T(8,128)(2,1)} %param.2, bf16[16,3,10240]{2,1,0:T(4,128)(2,1)S(1)} %all_gather.3, f32[3,64]{1,0:T(4,128)S(1)} %add_bitcast_fusion), kind=kOutput, calls=%fused_computation | convolution fusion | flops 125835264 | bytes 6882048 | tf_op jit(solution)/shard_map/lev,elw->vlw/dot_general | solution.py:20
  72.7 0.0 copy-start.1
  72.7 2.9 %copy.3 = f32[16,3,10240]{2,1,0:T(4,128)} copy(f32[16,3,10240]{2,0,1:T(8,128)S(1)} %convolution_bitcast_fusion) | data formatting | bytes 3932160 | tf_op jit(solution)/shard_map/lev,elw->vlw/transpose | solution.py:20
  75.5 0.0 all-reduce.3.cloned.1.call-update
  75.6 0.0 copy-done.1
  75.6 0.6 dynamic-slice
  76.2 97.5 %all-reduce.3.cloned.1.call-done = f32[16,3,10240]{2,1,0:T(4,128)} async-done(((f32[16,3,10240]{2,1,0:T(4,128)}), f32[16,3,10240]{2,1,0:T(4,128)}) %all-reduce.3.cloned.1.call-update) | async-done | bytes 1966096
  173.7 1.6 constant_dynamic-slice_fusion
  175.3 0.8 copy.4
  (1 shorter events, 0.0 us)
Async XLA Ops:
  6.5 38.3 %copy-start = (bf16[1,3,10240]{2,1,0:T(4,128)(2,1)S(1)}, bf16[1,3,10240]{2,1,0:T(4,128)(2,1)}, u32[]{:S(2)}) copy-start(bf16[1,3,10240]{2,1,0:T(4,128)(2,1)} %param.3) | copy-start | bytes 184324
  6.5 167.1 %all-reduce.3.cloned.1.call-start = ((), (), s32[]{:S(2)}) async-start(), calls=%async_computation | async-start | bytes 5242880
  72.7 2.9 %copy-start.1 = (u32[32]{0:T(128)S(1)}, u32[32]{0:T(128)}, u32[]{:S(2)}) copy-start(u32[32]{0:T(128)} %constant.11) | copy-start | bytes 388
Sparse Core Ops, SparseCore 0:
  75.7 97.9 all-reduce.2
where the time goes:
time: 183 us
  waiting for transfers between devices  97.5 us (53%)
  blocking collectives  57.8 us (32%)
  between operations  13.4 us (7%)
  local copies, waits for them, and re-layouts  5.84 us (3%)
  matrix products  5.1 us (3%)
  other arithmetic  3.22 us (2%)
    unnamed x2, waiting for transfers between devices  97.5 us
    psum x1, blocking collectives, shards(): total = lax.psum(jnp.sum(norms, axis=0), 'dp')  35 us
    all_gather x1, blocking collectives, shards(): everything = lax.all_gather(valid, 'dp', axis=0, tiled=True)  22.8 us
    dot_general x1, matrix products, shards(): jnp.einsum('lev,elw->vlw', coef, grads, preferred_element_type=jnp.float32)  5.1 us
  transfers between devices with their start and end apart: 1, of which 1 were waited for; matrix products, arithmetic and copies ran while one was open for 0% of the time, Pallas kernels for 0%

commit v1 on v0

--- a/solution.py
+++ b/solution.py
@@ -1,7 +1,14 @@
+import functools
+
 import jax
 import jax.numpy as jnp
 from jax import lax
+from jax.experimental import pallas as pl
+from jax.experimental.pallas import tpu as pltpu
 from jax.sharding import PartitionSpec as P
+
+MESH = pl.DeviceIdType.MESH
+LANES = 128
 
 
 def coefficients(grads, block, damping, norms):
@@ -24,9 +31,264 @@
     )
 
 
+NC, NY, NZ = 2, 2, 4
+N = NC * NY * NZ
+HALF = NY * NZ
+
+
+def slot(dc, dy, dz):
+    return (dc * NY + dy) * NZ + dz % NZ
+
+
+def kernel(
+    grads_hbm, valid_ref, out_ref,
+    grads, row_form, everything, v_form, norms, total, totals, partial, from_core, to_y, from_y, to_z, from_z, mine,
+    load_sem, gather_send, gather_recv, total_send, total_recv,
+    core_send, core_recv, y_send, y_recv, z_send, z_recv,
+):
+    layers, examples, width = grads_hbm.shape
+    chunks = width // LANES
+    part, me = lax.axis_index("parts"), lax.axis_index("dp")
+    c, y, z = me % NC, (me // NC) % NY, me // (NC * NY)
+
+    def device(dc, dy, dz):
+        pc = 1 - c if dc else c
+        py = 1 - y if dy else y
+        pz = (z + dz) % NZ
+        return (part, (pz * NY + py) * NC + pc)
+
+    def copy(src, dst, send, recv, to):
+        return pltpu.make_async_remote_copy(
+            src_ref=src, dst_ref=dst, send_sem=send, recv_sem=recv, device_id=to, device_id_type=MESH
+        )
+
+    sent = []
+
+    def start(*args):
+        one = copy(*args)
+        one.start()
+        sent.append(one)
+
+    offsets = [(dc, dy, dz) for dc in range(NC) for dy in range(NY) for dz in range(NZ) if (dc, dy, dz) != (0, 0, 0)]
+
+    loads = [pltpu.make_async_copy(grads_hbm.at[l], grads.at[l], load_sem.at[l]) for l in range(layers)]
+    for load in loads:
+        load.start()
+
+    barrier = pltpu.get_barrier_semaphore()
+    for offset in offsets:
+        pl.semaphore_signal(barrier, inc=1, device_id=device(*offset), device_id_type=MESH)
+
+    for j in range(chunks):
+        row_form[8 * j : 8 * j + layers, :] = valid_ref[:, LANES * j : LANES * (j + 1)].astype(jnp.float32)
+    for l in range(layers):
+        everything[l, 0] = row_form[pl.ds(l, chunks, stride=8), :].astype(jnp.bfloat16)
+    pl.semaphore_wait(barrier, N - 1)
+
+    counter = [0] * layers
+
+    def give(l, src, dst, to):
+        start(everything.at[l, src], everything.at[l, dst], gather_send.at[l, counter[l]], gather_recv.at[l, dst], to)
+        counter[l] += 1
+
+    arrived = set()
+
+    def take(l, k):
+        if (l, k) not in arrived:
+            arrived.add((l, k))
+            copy(
+                everything.at[l, k], everything.at[l, k], gather_send.at[l, 0], gather_recv.at[l, k], device(1, 0, 0)
+            ).wait_recv()
+
+    def gather_1(l):
+        for dz in (2, 1, 3):
+            give(l, 0, slot(0, 0, -dz), device(0, 0, dz))
+        give(l, 0, slot(0, 1, 0), device(0, 1, 0))
+        give(l, 0, slot(1, 0, 0), device(1, 0, 0))
+
+    def gather_2(l):
+        for dz in (1, 3, 2):
+            k = slot(0, 0, dz)
+            take(l, k)
+            give(l, k, slot(0, 1, dz), device(0, 1, 0))
+            give(l, k, slot(1, 0, dz), device(1, 0, 0))
+
+    def gather_3(l):
+        for dz in (0, 1, 3, 2):
+            k = slot(0, 1, dz)
+            take(l, k)
+            give(l, k, slot(1, 1, dz), device(1, 0, 0))
+
+    def norm(l):
+        loads[l].wait()
+        wide = 8 * LANES if width % (8 * LANES) == 0 else LANES
+
+        def body(i, acc):
+            x = grads[l, :, pl.ds(pl.multiple_of(i * wide, wide), wide)].astype(jnp.float32)
+            x = x * x
+            for j in range(wide // LANES):
+                acc = acc + x[:, LANES * j : LANES * (j + 1)]
+            return acc
+
+        acc = lax.fori_loop(0, width // wide, body, jnp.zeros((examples, LANES), jnp.float32))
+        each = jnp.sum(acc, axis=1, keepdims=True)
+        norms[l] = jnp.broadcast_to(each, (examples, LANES))
+        total[l : l + 1, :] = jnp.broadcast_to(jnp.sum(each, axis=0, keepdims=True), (1, LANES))
+
+    def send_totals():
+        for dc, dy, dz in offsets:
+            k = slot(dc, dy, -dz)
+            start(total, totals.at[k], total_send.at[k], total_recv.at[k], device(dc, dy, dz))
+
+    def take_totals():
+        for dc, dy, dz in offsets:
+            k = slot(dc, dy, dz)
+            copy(total, totals.at[k], total_send.at[k], total_recv.at[k], device(1, 0, 0)).wait_recv()
+        acc = total[...]
+        for dc, dy, dz in offsets:
+            acc = acc + totals[slot(dc, dy, dz)]
+        total_damping = 0.1 * acc / (examples * N)
+        return total_damping
+
+    def form(l):
+        for k in range(N):
+            if k:
+                take(l, k)
+            v_form[pl.ds(k, chunks, stride=N), :] = everything[l, k].astype(jnp.float32)
+
+    def dots(l):
+        wide = 2560 if width % 2560 == 0 else width
+        acc = jnp.zeros((examples, N), jnp.float32)
+        for i in range(width // wide):
+            block = jnp.concatenate(
+                [v_form[N * j : N * (j + 1), :] for j in range(i * wide // LANES, (i + 1) * wide // LANES)], axis=1
+            ).astype(jnp.bfloat16)
+            acc = acc + lax.dot_general(
+                grads[l, :, i * wide : (i + 1) * wide], block, (((1,), (1,)), ((), ())),
+                preferred_element_type=jnp.float32,
+            )
+        return acc
+
+    def weigh(l, product, damping):
+        coef = product / (damping[l : l + 1, :N] + norms[l, :, :N])
+        coef = coef.T.astype(jnp.bfloat16)
+        wide = 1280 if width % 1280 == 0 else width
+        for i in range(width // wide):
+            result = jnp.dot(coef, grads[l, :, i * wide : (i + 1) * wide], preferred_element_type=jnp.float32)
+            for j in range(wide // LANES):
+                at = i * wide // LANES + j
+                for dc in range(NC):
+                    partial[l, dc, HALF * at : HALF * (at + 1), :] = result[HALF * dc : HALF * (dc + 1), LANES * j : LANES * (j + 1)]
+        start(partial.at[l, 1], from_core.at[l], core_send.at[l], core_recv.at[l], device(1, 0, 0))
+
+    def scatter_y(l):
+        copy(partial.at[l, 1], from_core.at[l], core_send.at[l], core_recv.at[l], device(1, 0, 0)).wait_recv()
+        for dz in range(NZ):
+            rows = pl.ds(slot(0, 1, dz), chunks, stride=HALF)
+            to_y[l, dz] = (partial[l, 0, rows, :] + from_core[l, rows, :]).astype(jnp.bfloat16)
+        start(to_y.at[l], from_y.at[l], y_send.at[l], y_recv.at[l], device(0, 1, 0))
+
+    def scatter_z(l):
+        copy(to_y.at[l], from_y.at[l], y_send.at[l], y_recv.at[l], device(0, 1, 0)).wait_recv()
+        for dz in (2, 1, 3, 0):
+            rows = pl.ds(slot(0, 0, dz), chunks, stride=HALF)
+            part_sum = partial[l, 0, rows, :] + from_core[l, rows, :] + from_y[l, dz].astype(jnp.float32)
+            if dz:
+                to_z[l, dz - 1] = part_sum.astype(jnp.bfloat16)
+                at = NZ - dz - 1
+                start(to_z.at[l, dz - 1], from_z.at[l, at], z_send.at[l, dz - 1], z_recv.at[l, at], device(0, 0, dz))
+            else:
+                mine[l] = part_sum
+
+    def finish(l):
+        acc = mine[l]
+        for i in range(NZ - 1):
+            copy(to_z.at[l, i], from_z.at[l, i], z_send.at[l, i], z_recv.at[l, i], device(0, 1, 0)).wait_recv()
+            acc = acc + from_z[l, i].astype(jnp.float32)
+        out_ref[l] = acc
+
+    total[...] = jnp.zeros_like(total)
+    for l in range(layers):
+        gather_1(l)
+    for l in range(layers):
+        norm(l)
+        gather_2(l)
+        if l:
+            gather_3(l - 1)
+    send_totals()
+    damping = None
+    for l in range(layers):
+        form(l)
+        product = dots(l)
+        if l == 0:
+            damping = take_totals()
+        weigh(l, product, damping)
+        if l == 0:
+            gather_3(layers - 1)
+        if l >= 1:
+            scatter_y(l - 1)
+        if l >= 2:
+            scatter_z(l - 2)
+    scatter_y(layers - 1)
+    for l in range(max(layers - 2, 0), layers):
+        scatter_z(l)
+    for l in range(layers):
+        finish(l)
+    for one in sent:
+        one.wait_send()
+
+
+def fused(grads, valid):
+    examples, layers, width = grads.shape
+    chunks = width // LANES
+    bf16, f32 = jnp.bfloat16, jnp.float32
+    dma = pltpu.SemaphoreType.DMA
+    out = pl.pallas_call(
+        kernel,
+        out_shape=jax.ShapeDtypeStruct((layers, chunks, LANES), f32),
+        in_specs=[pl.BlockSpec(memory_space=pl.ANY), pl.BlockSpec(memory_space=pltpu.VMEM)],
+        out_specs=pl.BlockSpec(memory_space=pltpu.VMEM),
+        scratch_shapes=[
+            pltpu.VMEM((layers, examples, width), bf16),
+            pltpu.VMEM((chunks * 8, LANES), f32),
+            pltpu.VMEM((layers, N, chunks, LANES), bf16),
+            pltpu.VMEM((chunks * N, LANES), f32),
+            pltpu.VMEM((layers, examples, LANES), f32),
+            pltpu.VMEM((8, LANES), f32),
+            pltpu.VMEM((N, 8, LANES), f32),
+            pltpu.VMEM((layers, NC, chunks * HALF, LANES), f32),
+            pltpu.VMEM((layers, chunks * HALF, LANES), f32),
+            pltpu.VMEM((layers, NZ, chunks, LANES), bf16),
+            pltpu.VMEM((layers, NZ, chunks, LANES), bf16),
+            pltpu.VMEM((layers, NZ - 1, chunks, LANES), bf16),
+            pltpu.VMEM((layers, NZ - 1, chunks, LANES), bf16),
+            pltpu.VMEM((layers, chunks, LANES), f32),
+            dma((layers,)),
+            dma((layers, N)),
+            dma((layers, N)),
+            dma((N,)),
+            dma((N,)),
+            dma((layers,)),
+            dma((layers,)),
+            dma((layers,)),
+            dma((layers,)),
+            dma((layers, NZ - 1)),
+            dma((layers, NZ - 1)),
+        ],
+        compiler_params=pltpu.CompilerParams(
+            collective_id=0, has_side_effects=True, vmem_limit_bytes=48 * 1024 * 1024
+        ),
+    )(jnp.transpose(grads, (1, 0, 2)), valid.reshape(layers, width))
+    return out.reshape(1, layers, width)
+
+
 def solution(mesh):
+    def step(grads, valid):
+        fits = mesh.shape["dp"] == N and valid.shape[0] == 1 and grads.shape[2] % (16 * LANES) == 0
+        return (fused if fits else shards)(grads, valid)
+
     return jax.shard_map(
-        shards,
+        step,
         mesh=mesh,
         in_specs=(P(("parts", "dp"), None, None), P(("parts", "dp"), None, None)),
         out_specs=P(("parts", "dp"), None, None),

time: 183 us -> 38.4 us (0.21)
  waiting for transfers between devices: 97.5 us -> 0 us
  blocking collectives: 57.8 us -> 0 us
  Pallas kernels: 0 us -> 34.5 us
  between operations: 13.4 us -> 0.01 us
  matrix products: 5.1 us -> 0 us
  other arithmetic: 3.22 us -> 0 us
  local copies, waits for them, and re-layouts: 5.84 us -> 3.65 us
    unnamed x2 -> x0, waiting for transfers between devices: 97.5 us -> none
    psum x1 -> x0, blocking collectives: 35 us -> none  [shards(): total = lax.psum(jnp.sum(norms, axis=0), 'dp')]
    pallas_call x0 -> x1, Pallas kernels: none -> 34.5 us  [fused(): pl.pallas_call(kernel, out_shape=jax.ShapeDtypeStruct((layers, chunks, LA...]
    all_gather x1 -> x0, blocking collectives: 22.8 us -> none  [shards(): everything = lax.all_gather(valid, 'dp', axis=0, tiled=True)]
    dot_general x1 -> x0, matrix products: 5.1 us -> none  [shards(): jnp.einsum('lev,elw->vlw', coef, grads, preferred_element_type=jnp.float32)]
    dot_general x1 -> x0, other arithmetic: 3.02 us -> none  [shards(): jnp.einsum('elw,elw->el', grads, grads, preferred_element_type=jnp.float32)]
    transpose x1 -> x0, local copies, waits for them, and re-layouts: 2.88 us -> none  [shards(): jnp.einsum('lev,elw->vlw', coef, grads, preferred_element_type=jnp.float32)]
  transfers between devices with their start and end apart: 1 -> 0, of which waited for: 1 -> 0; matrix products, arithmetic and copies ran while one was open for 0% -> 0% of each run, Pallas kernels for 0% -> 0%
where the time goes in v1:
time: 38.4 us; the launch traced here: 38.2 us
  Pallas kernels  34.5 us (90%)
  local copies, waits for them, and re-layouts  3.65 us (10%)
    pallas_call x1, Pallas kernels, fused(): pl.pallas_call(kernel, out_shape=jax.ShapeDtypeStruct((layers, chunks, LA...  34.5 us
    unnamed x5, local copies, waits for them, and re-layouts  3.65 us

profile of v1, /device:TPU:0, one launch (start us, length us, event | category | flops | bytes accessed | tf_op | source)
XLA Modules:
  0.0 38.2 jit_solution(1837301443468943124)
XLA Ops:
  0.0 0.0 copy-start
  0.0 2.1 %copy-done = bf16[64,3,10240]{2,0,1:T(8,128)(2,1)S(1)} copy-done((bf16[64,3,10240]{2,0,1:T(8,128)(2,1)S(1)}, bf16[64,3,10240]{2,0,1:T(8,128)(2,1)}, u32[]{:S(2)}) %copy-start) | copy-done | bytes 3932184
  2.1 0.0 copy-start.1
  2.1 0.9 %copy-done.1 = bf16[1,3,10240]{2,1,0:T(4,128)(2,1)S(1)} copy-done((bf16[1,3,10240]{2,1,0:T(4,128)(2,1)S(1)}, bf16[1,3,10240]{2,1,0:T(4,128)(2,1)}, u32[]{:S(2)}) %copy-start.1) | copy-done | bytes 61464
  3.0 34.5 %shard_map.28 = f32[3,80,128]{2,1,0:T(8,128)S(1)} custom-call(bf16[3,64,10240]{2,1,0:T(8,128)(2,1)S(1)} %bitcast.3, bf16[3,10240]{1,0:T(4,128)(2,1)S(1)} %bitcast.5), custom_call_target="tpu_custom_call" | custom-call | tf_op jit(solution)/shard_map/pallas_call | solution.py:246
  37.5 0.7 %copy.6 = f32[1,3,10240]{2,0,1:T(1,128)} copy(f32[1,3,10240]{2,0,1:T(1,128)S(1)} %bitcast.4) | data formatting | bytes 245760
Async XLA Ops:
  0.0 2.1 %copy-start = (bf16[64,3,10240]{2,0,1:T(8,128)(2,1)S(1)}, bf16[64,3,10240]{2,0,1:T(8,128)(2,1)}, u32[]{:S(2)}) copy-start(bf16[64,3,10240]{2,0,1:T(8,128)(2,1)} %param.2) | copy-start | bytes 11796484
  2.1 0.9 %copy-start.1 = (bf16[1,3,10240]{2,1,0:T(4,128)(2,1)S(1)}, bf16[1,3,10240]{2,1,0:T(4,128)(2,1)}, u32[]{:S(2)}) copy-start(bf16[1,3,10240]{2,1,0:T(4,128)(2,1)} %param.3) | copy-start | bytes 184324

commit v2 on v1

--- a/solution.py
+++ b/solution.py
@@ -41,9 +41,9 @@
 
 
 def kernel(
-    grads_hbm, valid_ref, out_ref,
-    grads, row_form, everything, v_form, norms, total, totals, partial, from_core, to_y, from_y, to_z, from_z, mine,
-    load_sem, gather_send, gather_recv, total_send, total_recv,
+    grads_hbm, valid_hbm, out_ref,
+    grads, valid_ref, row_form, everything, v_form, norms, total, totals, partial, from_core, to_y, from_y, to_z, from_z, mine,
+    load_sem, valid_sem, gather_send, gather_recv, total_send, total_recv,
     core_send, core_recv, y_send, y_recv, z_send, z_recv,
 ):
     layers, examples, width = grads_hbm.shape
@@ -71,19 +71,21 @@
 
     offsets = [(dc, dy, dz) for dc in range(NC) for dy in range(NY) for dz in range(NZ) if (dc, dy, dz) != (0, 0, 0)]
 
+    barrier = pltpu.get_barrier_semaphore()
+    for offset in offsets:
+        pl.semaphore_signal(barrier, inc=1, device_id=device(*offset), device_id_type=MESH)
+
+    load_valid = pltpu.make_async_copy(valid_hbm, valid_ref, valid_sem)
+    load_valid.start()
     loads = [pltpu.make_async_copy(grads_hbm.at[l], grads.at[l], load_sem.at[l]) for l in range(layers)]
     for load in loads:
         load.start()
 
-    barrier = pltpu.get_barrier_semaphore()
-    for offset in offsets:
-        pl.semaphore_signal(barrier, inc=1, device_id=device(*offset), device_id_type=MESH)
-
+    load_valid.wait()
     for j in range(chunks):
         row_form[8 * j : 8 * j + layers, :] = valid_ref[:, LANES * j : LANES * (j + 1)].astype(jnp.float32)
     for l in range(layers):
         everything[l, 0] = row_form[pl.ds(l, chunks, stride=8), :].astype(jnp.bfloat16)
-    pl.semaphore_wait(barrier, N - 1)
 
     counter = [0] * layers
 
@@ -133,7 +135,7 @@
         acc = lax.fori_loop(0, width // wide, body, jnp.zeros((examples, LANES), jnp.float32))
         each = jnp.sum(acc, axis=1, keepdims=True)
         norms[l] = jnp.broadcast_to(each, (examples, LANES))
-        total[l : l + 1, :] = jnp.broadcast_to(jnp.sum(each, axis=0, keepdims=True), (1, LANES))
+        return jnp.broadcast_to(jnp.sum(each, axis=0, keepdims=True), (1, LANES))
 
     def send_totals():
         for dc, dy, dz in offsets:
@@ -170,7 +172,7 @@
         return acc
 
     def weigh(l, product, damping):
-        coef = product / (damping[l : l + 1, :N] + norms[l, :, :N])
+        coef = product / (damping[:, l : l + 1] + norms[l, :, :N])
         coef = coef.T.astype(jnp.bfloat16)
         wide = 1280 if width % 1280 == 0 else width
         for i in range(width // wide):
@@ -207,15 +209,20 @@
             acc = acc + from_z[l, i].astype(jnp.float32)
         out_ref[l] = acc
 
-    total[...] = jnp.zeros_like(total)
-    for l in range(layers):
+    lane = lax.broadcasted_iota(jnp.int32, (1, LANES), 1)
+    row = jnp.zeros((1, LANES), jnp.float32)
+    for l in range(layers):
+        row = jnp.where(lane == l, norm(l), row)
+    total[...] = row
+    pl.semaphore_wait(barrier, N - 1)
+    gather_1(0)
+    send_totals()
+    for l in range(1, layers):
         gather_1(l)
     for l in range(layers):
-        norm(l)
         gather_2(l)
         if l:
             gather_3(l - 1)
-    send_totals()
     damping = None
     for l in range(layers):
         form(l)
@@ -246,16 +253,17 @@
     out = pl.pallas_call(
         kernel,
         out_shape=jax.ShapeDtypeStruct((layers, chunks, LANES), f32),
-        in_specs=[pl.BlockSpec(memory_space=pl.ANY), pl.BlockSpec(memory_space=pltpu.VMEM)],
+        in_specs=[pl.BlockSpec(memory_space=pl.ANY), pl.BlockSpec(memory_space=pl.ANY)],
         out_specs=pl.BlockSpec(memory_space=pltpu.VMEM),
         scratch_shapes=[
             pltpu.VMEM((layers, examples, width), bf16),
+            pltpu.VMEM((layers, width), bf16),
             pltpu.VMEM((chunks * 8, LANES), f32),
             pltpu.VMEM((layers, N, chunks, LANES), bf16),
             pltpu.VMEM((chunks * N, LANES), f32),
             pltpu.VMEM((layers, examples, LANES), f32),
-            pltpu.VMEM((8, LANES), f32),
-            pltpu.VMEM((N, 8, LANES), f32),
+            pltpu.VMEM((1, LANES), f32),
+            pltpu.VMEM((N, 1, LANES), f32),
             pltpu.VMEM((layers, NC, chunks * HALF, LANES), f32),
             pltpu.VMEM((layers, chunks * HALF, LANES), f32),
             pltpu.VMEM((layers, NZ, chunks, LANES), bf16),
@@ -264,6 +272,7 @@
             pltpu.VMEM((layers, NZ - 1, chunks, LANES), bf16),
             pltpu.VMEM((layers, chunks, LANES), f32),
             dma((layers,)),
+            dma,
             dma((layers, N)),
             dma((layers, N)),
             dma((N,)),
@@ -276,7 +285,7 @@
             dma((layers, NZ - 1)),
         ],
         compiler_params=pltpu.CompilerParams(
-            collective_id=0, has_side_effects=True, vmem_limit_bytes=48 * 1024 * 1024
+            collective_id=0, has_side_effects=True, vmem_limit_bytes=60 * 1024 * 1024
         ),
     )(jnp.transpose(grads, (1, 0, 2)), valid.reshape(layers, width))
     return out.reshape(1, layers, width)

time: 38.4 us -> 34 us (0.89)
  Pallas kernels: 34.5 us -> 32.3 us
  local copies, waits for them, and re-layouts: 3.65 us -> 1.56 us
    pallas_call x1, Pallas kernels: 34.5 us -> 32.3 us  [fused(): pl.pallas_call(kernel, out_shape=jax.ShapeDtypeStruct((layers, chunks, LA...]
    unnamed x5 -> x1, local copies, waits for them, and re-layouts: 3.65 us -> 1.56 us
where the time goes in v2:
time: 34 us; the launch traced here: 33.9 us
  Pallas kernels  32.3 us (95%)
  local copies, waits for them, and re-layouts  1.56 us (5%)
    pallas_call x1, Pallas kernels, fused(): pl.pallas_call(kernel, out_shape=jax.ShapeDtypeStruct((layers, chunks, LA...  32.3 us
    unnamed x1, local copies, waits for them, and re-layouts  1.56 us

profile of v2, /device:TPU:0, one launch (start us, length us, event | category | flops | bytes accessed | tf_op | source)
XLA Modules:
  0.0 33.9 jit_solution(4461086419530129290)
XLA Ops:
  0.0 32.3 %shard_map.28 = f32[3,80,128]{2,1,0:T(8,128)} custom-call(bf16[3,64,10240]{2,1,0:T(8,128)(2,1)} %bitcast.3, bf16[3,10240]{1,0:T(4,128)(2,1)} %bitcast.5), custom_call_target="tpu_custom_call" | custom-call | tf_op jit(solution)/shard_map/pallas_call | solution.py:253
  32.3 1.6 %copy.6 = f32[1,3,10240]{2,0,1:T(1,128)} copy(f32[1,3,10240]{2,0,1:T(1,128)} %bitcast.4) | data formatting | bytes 245760

commit v3 on v2

--- a/solution.py
+++ b/solution.py
@@ -69,7 +69,7 @@
         one.start()
         sent.append(one)
 
-    offsets = [(dc, dy, dz) for dc in range(NC) for dy in range(NY) for dz in range(NZ) if (dc, dy, dz) != (0, 0, 0)]
+    offsets = [(0, 0, dz) for dz in (2, 1, 3)] + [(0, 1, 0), (1, 0, 0)]
 
     barrier = pltpu.get_barrier_semaphore()
     for offset in offsets:
@@ -103,7 +103,7 @@
             ).wait_recv()
 
     def gather_1(l):
-        for dz in (2, 1, 3):
+        for dz in (1, 3, 2):
             give(l, 0, slot(0, 0, -dz), device(0, 0, dz))
         give(l, 0, slot(0, 1, 0), device(0, 1, 0))
         give(l, 0, slot(1, 0, 0), device(1, 0, 0))
@@ -137,20 +137,28 @@
         norms[l] = jnp.broadcast_to(each, (examples, LANES))
         return jnp.broadcast_to(jnp.sum(each, axis=0, keepdims=True), (1, LANES))
 
-    def send_totals():
-        for dc, dy, dz in offsets:
-            k = slot(dc, dy, -dz)
-            start(total, totals.at[k], total_send.at[k], total_recv.at[k], device(dc, dy, dz))
+    def totals_z():
+        for dz in (2, 1, 3):
+            at = NZ - dz - 1
+            start(total.at[0], totals.at[at], total_send.at[dz - 1], total_recv.at[at], device(0, 0, dz))
+
+    def add_totals(step, first, count):
+        acc = total[step]
+        for i in range(first, first + count):
+            copy(total.at[0], totals.at[i], total_send.at[i], total_recv.at[i], device(0, 1, 0)).wait_recv()
+            acc = acc + totals[i]
+        return acc
+
+    def totals_y():
+        total[1] = add_totals(0, 0, NZ - 1)
+        start(total.at[1], totals.at[NZ - 1], total_send.at[NZ - 1], total_recv.at[NZ - 1], device(0, 1, 0))
+
+    def totals_core():
+        total[2] = add_totals(1, NZ - 1, 1)
+        start(total.at[2], totals.at[NZ], total_send.at[NZ], total_recv.at[NZ], device(1, 0, 0))
 
     def take_totals():
-        for dc, dy, dz in offsets:
-            k = slot(dc, dy, dz)
-            copy(total, totals.at[k], total_send.at[k], total_recv.at[k], device(1, 0, 0)).wait_recv()
-        acc = total[...]
-        for dc, dy, dz in offsets:
-            acc = acc + totals[slot(dc, dy, dz)]
-        total_damping = 0.1 * acc / (examples * N)
-        return total_damping
+        return 0.1 * add_totals(2, NZ, 1) / (examples * N)
 
     def form(l):
         for k in range(N):
@@ -185,14 +193,16 @@
 
     def scatter_y(l):
         copy(partial.at[l, 1], from_core.at[l], core_send.at[l], core_recv.at[l], device(1, 0, 0)).wait_recv()
-        for dz in range(NZ):
+        for dz in (2, 1, 3, 0):
             rows = pl.ds(slot(0, 1, dz), chunks, stride=HALF)
             to_y[l, dz] = (partial[l, 0, rows, :] + from_core[l, rows, :]).astype(jnp.bfloat16)
-        start(to_y.at[l], from_y.at[l], y_send.at[l], y_recv.at[l], device(0, 1, 0))
+            start(to_y.at[l, dz], from_y.at[l, dz], y_send.at[l, dz], y_recv.at[l, dz], device(0, 1, 0))
 
     def scatter_z(l):
-        copy(to_y.at[l], from_y.at[l], y_send.at[l], y_recv.at[l], device(0, 1, 0)).wait_recv()
         for dz in (2, 1, 3, 0):
+            copy(
+                to_y.at[l, dz], from_y.at[l, dz], y_send.at[l, dz], y_recv.at[l, dz], device(0, 1, 0)
+            ).wait_recv()
             rows = pl.ds(slot(0, 0, dz), chunks, stride=HALF)
             part_sum = partial[l, 0, rows, :] + from_core[l, rows, :] + from_y[l, dz].astype(jnp.float32)
             if dz:
@@ -213,27 +223,30 @@
     row = jnp.zeros((1, LANES), jnp.float32)
     for l in range(layers):
         row = jnp.where(lane == l, norm(l), row)
-    total[...] = row
-    pl.semaphore_wait(barrier, N - 1)
+    total[0] = row
+    pl.semaphore_wait(barrier, len(offsets))
     gather_1(0)
-    send_totals()
+    totals_z()
     for l in range(1, layers):
         gather_1(l)
-    for l in range(layers):
+    gather_2(0)
+    totals_y()
+    for l in range(1, layers):
         gather_2(l)
-        if l:
-            gather_3(l - 1)
+        gather_3(l - 1)
+        if l == 1:
+            totals_core()
     damping = None
     for l in range(layers):
         form(l)
         product = dots(l)
         if l == 0:
             damping = take_totals()
+        else:
+            scatter_y(l - 1)
         weigh(l, product, damping)
         if l == 0:
             gather_3(layers - 1)
-        if l >= 1:
-            scatter_y(l - 1)
         if l >= 2:
             scatter_z(l - 2)
     scatter_y(layers - 1)
@@ -262,8 +275,8 @@
             pltpu.VMEM((layers, N, chunks, LANES), bf16),
             pltpu.VMEM((chunks * N, LANES), f32),
             pltpu.VMEM((layers, examples, LANES), f32),
-            pltpu.VMEM((1, LANES), f32),
-            pltpu.VMEM((N, 1, LANES), f32),
+            pltpu.VMEM((3, 1, LANES), f32),
+            pltpu.VMEM((NZ + 1, 1, LANES), f32),
             pltpu.VMEM((layers, NC, chunks * HALF, LANES), f32),
             pltpu.VMEM((layers, chunks * HALF, LANES), f32),
             pltpu.VMEM((layers, NZ, chunks, LANES), bf16),
@@ -275,12 +288,12 @@
             dma,
             dma((layers, N)),
             dma((layers, N)),
-            dma((N,)),
-            dma((N,)),
+            dma((NZ + 1,)),
+            dma((NZ + 1,)),
             dma((layers,)),
             dma((layers,)),
-            dma((layers,)),
-            dma((layers,)),
+            dma((layers, NZ)),
+            dma((layers, NZ)),
             dma((layers, NZ - 1)),
             dma((layers, NZ - 1)),
         ],

time: 34 us -> 33.2 us (0.976)
  Pallas kernels: 32.3 us -> 31.5 us
    pallas_call x1, Pallas kernels: 32.3 us -> 31.5 us  [fused(): pl.pallas_call(kernel, out_shape=jax.ShapeDtypeStruct((layers, chunks, LA...]
where the time goes in v3:
time: 33.2 us; the launch traced here: 33.1 us
  Pallas kernels  31.5 us (95%)
  local copies, waits for them, and re-layouts  1.56 us (5%)
    pallas_call x1, Pallas kernels, fused(): pl.pallas_call(kernel, out_shape=jax.ShapeDtypeStruct((layers, chunks, LA...  31.5 us
    unnamed x1, local copies, waits for them, and re-layouts  1.56 us

profile of v3, /device:TPU:0, one launch (start us, length us, event | category | flops | bytes accessed | tf_op | source)
XLA Modules:
  0.0 33.1 jit_solution(15227468886702684561)
XLA Ops:
  0.0 31.5 %shard_map.28 = f32[3,80,128]{2,1,0:T(8,128)} custom-call(bf16[3,64,10240]{2,1,0:T(8,128)(2,1)} %bitcast.3, bf16[3,10240]{1,0:T(4,128)(2,1)} %bitcast.5), custom_call_target="tpu_custom_call" | custom-call | tf_op jit(solution)/shard_map/pallas_call | solution.py:266
  31.5 1.6 %copy.6 = f32[1,3,10240]{2,0,1:T(1,128)} copy(f32[1,3,10240]{2,0,1:T(1,128)} %bitcast.4) | data formatting | bytes 245760

commit v4 on v3

--- a/solution.py
+++ b/solution.py
@@ -193,13 +193,13 @@
 
     def scatter_y(l):
         copy(partial.at[l, 1], from_core.at[l], core_send.at[l], core_recv.at[l], device(1, 0, 0)).wait_recv()
-        for dz in (2, 1, 3, 0):
+        for dz in (3, 1, 2, 0):
             rows = pl.ds(slot(0, 1, dz), chunks, stride=HALF)
             to_y[l, dz] = (partial[l, 0, rows, :] + from_core[l, rows, :]).astype(jnp.bfloat16)
             start(to_y.at[l, dz], from_y.at[l, dz], y_send.at[l, dz], y_recv.at[l, dz], device(0, 1, 0))
 
     def scatter_z(l):
-        for dz in (2, 1, 3, 0):
+        for dz in (3, 1, 2, 0):
             copy(
                 to_y.at[l, dz], from_y.at[l, dz], y_send.at[l, dz], y_recv.at[l, dz], device(0, 1, 0)
             ).wait_recv()
@@ -221,11 +221,11 @@
 
     lane = lax.broadcasted_iota(jnp.int32, (1, LANES), 1)
     row = jnp.zeros((1, LANES), jnp.float32)
-    for l in range(layers):
+    for l in range(layers - 1):
         row = jnp.where(lane == l, norm(l), row)
-    total[0] = row
     pl.semaphore_wait(barrier, len(offsets))
     gather_1(0)
+    total[0] = jnp.where(lane == layers - 1, norm(layers - 1), row)
     totals_z()
     for l in range(1, layers):
         gather_1(l)

time: 33.2 us -> 32.6 us (0.982)
  Pallas kernels: 31.5 us -> 30.9 us
    pallas_call x1, Pallas kernels: 31.5 us -> 30.9 us  [fused(): pl.pallas_call(kernel, out_shape=jax.ShapeDtypeStruct((layers, chunks, LA...]
where the time goes in v4:
time: 32.6 us; the launch traced here: 32.5 us
  Pallas kernels  30.9 us (95%)
  local copies, waits for them, and re-layouts  1.56 us (5%)
    pallas_call x1, Pallas kernels, fused(): pl.pallas_call(kernel, out_shape=jax.ShapeDtypeStruct((layers, chunks, LA...  30.9 us
    unnamed x1, local copies, waits for them, and re-layouts  1.56 us

profile of v4, /device:TPU:0, one launch (start us, length us, event | category | flops | bytes accessed | tf_op | source)
XLA Modules:
  0.0 32.5 jit_solution(1356095602883450902)
XLA Ops:
  0.0 30.9 %shard_map.28 = f32[3,80,128]{2,1,0:T(8,128)} custom-call(bf16[3,64,10240]{2,1,0:T(8,128)(2,1)} %bitcast.3, bf16[3,10240]{1,0:T(4,128)(2,1)} %bitcast.5), custom_call_target="tpu_custom_call" | custom-call | tf_op jit(solution)/shard_map/pallas_call | solution.py:266
  30.9 1.6 %copy.6 = f32[1,3,10240]{2,0,1:T(1,128)} copy(f32[1,3,10240]{2,0,1:T(1,128)} %bitcast.4) | data formatting | bytes 245760

commit v5 on v4

--- a/solution.py
+++ b/solution.py
@@ -242,9 +242,9 @@
         product = dots(l)
         if l == 0:
             damping = take_totals()
-        else:
+        weigh(l, product, damping)
+        if l:
             scatter_y(l - 1)
-        weigh(l, product, damping)
         if l == 0:
             gather_3(layers - 1)
         if l >= 2:

time: 32.6 us -> 32.5 us (level)
  no operation moved by 1% of the time
where the time goes in v5:
time: 32.5 us; the launch traced here: 32.4 us
  Pallas kernels  30.8 us (95%)
  local copies, waits for them, and re-layouts  1.56 us (5%)
    pallas_call x1, Pallas kernels, fused(): pl.pallas_call(kernel, out_shape=jax.ShapeDtypeStruct((layers, chunks, LA...  30.8 us
    unnamed x1, local copies, waits for them, and re-layouts  1.56 us

profile of v5, /device:TPU:0, one launch (start us, length us, event | category | flops | bytes accessed | tf_op | source)
XLA Modules:
  0.0 32.4 jit_solution(5679800223553389714)
XLA Ops:
  0.0 30.8 %shard_map.28 = f32[3,80,128]{2,1,0:T(8,128)} custom-call(bf16[3,64,10240]{2,1,0:T(8,128)(2,1)} %bitcast.3, bf16[3,10240]{1,0:T(4,128)(2,1)} %bitcast.5), custom_call_target="tpu_custom_call" | custom-call | tf_op jit(solution)/shard_map/pallas_call | solution.py:266
  30.8 1.6 %copy.6 = f32[1,3,10240]{2,0,1:T(1,128)} copy(f32[1,3,10240]{2,0,1:T(1,128)} %bitcast.4) | data formatting | bytes 245760

commit v6 on v5

--- a/solution.py
+++ b/solution.py
@@ -105,6 +105,8 @@
     def gather_1(l):
         for dz in (1, 3, 2):
             give(l, 0, slot(0, 0, -dz), device(0, 0, dz))
+
+    def gather_1_near(l):
         give(l, 0, slot(0, 1, 0), device(0, 1, 0))
         give(l, 0, slot(1, 0, 0), device(1, 0, 0))
 
@@ -225,6 +227,8 @@
         row = jnp.where(lane == l, norm(l), row)
     pl.semaphore_wait(barrier, len(offsets))
     gather_1(0)
+    for l in range(layers):
+        gather_1_near(l)
     total[0] = jnp.where(lane == layers - 1, norm(layers - 1), row)
     totals_z()
     for l in range(1, layers):

time: 32.5 us -> 32.4 us (level)
  no operation moved by 1% of the time
where the time goes in v6:
time: 32.4 us; the launch traced here: 32.3 us
  Pallas kernels  30.7 us (95%)
  local copies, waits for them, and re-layouts  1.56 us (5%)
    pallas_call x1, Pallas kernels, fused(): pl.pallas_call(kernel, out_shape=jax.ShapeDtypeStruct((layers, chunks, LA...  30.7 us
    unnamed x1, local copies, waits for them, and re-layouts  1.56 us

profile of v6, /device:TPU:0, one launch (start us, length us, event | category | flops | bytes accessed | tf_op | source)
XLA Modules:
  0.0 32.3 jit_solution(6741476702842039951)
XLA Ops:
  0.0 30.7 %shard_map.28 = f32[3,80,128]{2,1,0:T(8,128)} custom-call(bf16[3,64,10240]{2,1,0:T(8,128)(2,1)} %bitcast.3, bf16[3,10240]{1,0:T(4,128)(2,1)} %bitcast.5), custom_call_target="tpu_custom_call" | custom-call | tf_op jit(solution)/shard_map/pallas_call | solution.py:270
  30.7 1.6 %copy.6 = f32[1,3,10240]{2,0,1:T(1,128)} copy(f32[1,3,10240]{2,0,1:T(1,128)} %bitcast.4) | data formatting | bytes 245760
